TPU v7x, 32 devices: a whole 2x2x4 slice. The times are simulated.
32 devices in a mesh: region: 4 (over z), block: 8 (over y, x, core).
Axes of the slice: x: 2, y: 2, z: 4, core: 2. Of those that a mesh axis runs over, the one named last changes fastest.
Arguments:
- features: bfloat16 [128, 64, 512], P(('region', 'block')), may hold values from -6 to 6
- counts: int32 [128], P(('region', 'block')), may hold values from 0 to 512, as said below
- rebalance: int32 [128], P(('region', 'block')), may hold values from -1 to 63, as said below
- neighbors: int32 [128, 26], P(('region', 'block')), may hold values from -1 to 127, as said below
- coarse_owner: int32 [128], P(('region', 'block')), may hold values from -1 to 3, as said below
- conv_weight: bfloat16 [27, 64, 128], replicated, may hold values from -0.15625 to 0.15625
- convolution_bias_vector: float32 [128], replicated, may hold values from -3 to 3
- merged_adjoint: bfloat16 [64, 8192], P(('region', 'block')), may hold values from -0.119628906 to 0.119628906
Outputs:
- pooled: bfloat16 [64, 8192], P(('region', 'block'))
- weight_grad: float32 [27, 64, 128], replicated
- bias_grad: float32 [128], replicated
Inputs may be any that keep to these rules, and one draw needn't show every extreme that they name: `counts`: 0 marks an empty block; exactly half of each region group's blocks are occupied. `rebalance`: -1 for an empty block; else a row of the block's own region group, each row of a group taken by exactly one block; of the blocks of one device at most 1 have rows on one same device. `neighbors`: -1 where an offset has no occupied neighbour and at every offset of an empty block; neighbours at offsets with ea = 0 lie on the same device, the others on the same device or one of the two beside it along block in the same region group. `coarse_owner`: -1 for an empty block; of the blocks on one device of the working layout at most 1 have the same coarse owner.
All inputs are finite; a program needn't handle non-finite values.
Results may differ from a plain program's by a relative error of at most 0.0029.
Values may be sent and summed in bfloat16 or wider, within the bound.
A program may use at most 128 MiB of HBM per device.

v0:
```python
import functools
import math

import jax
import jax.numpy as jnp
from jax import lax
from jax.experimental import pallas as pl
from jax.experimental.pallas import tpu as pltpu
from jax.sharding import PartitionSpec as P

MESH = pl.DeviceIdType.MESH
VMEM_LIMIT = 48 * 1024 * 1024
F32 = jnp.float32
BF16 = jnp.bfloat16


def greet(region, block, regions, blocks):
    barrier = pltpu.get_barrier_semaphore()
    for k in range(1, blocks):
        pl.semaphore_signal(
            barrier, inc=1, device_id=(region, lax.rem(block + k, blocks)), device_id_type=MESH
        )
    for k in range(1, regions):
        pl.semaphore_signal(
            barrier, inc=1, device_id=(lax.rem(region + k, regions), block), device_id_type=MESH
        )
    pl.semaphore_wait(barrier, blocks + regions - 2)


def remote(src, dst, send_sem, recv_sem, device):
    return pltpu.make_async_remote_copy(
        src_ref=src,
        dst_ref=dst,
        send_sem=send_sem,
        recv_sem=recv_sem,
        device_id=device,
        device_id_type=MESH,
    )


def exchange_kernel(
    regions,
    blocks,
    counts_ref,
    rebalance_ref,
    owner_ref,
    features_ref,
    adjoint_ref,
    layers_ref,
    cotangent_ref,
    tags_ref,
    adjoints,
    outgoing,
    adj_send,
    adj_recv,
    tag_send,
    tag_recv,
    lay_send,
    lay_recv,
    cot_send,
    cot_recv,
):
    region, block = lax.axis_index("region"), lax.axis_index("block")
    home = features_ref.shape[0]
    work = adjoint_ref.shape[0]
    rows = lax.broadcasted_iota(jnp.int32, (blocks, 128), 0)
    codes = jnp.full((blocks, 128), -1, jnp.int32)
    for h in range(home):
        line = rebalance_ref[h]
        device = jnp.where(line >= 0, lax.rem(lax.div(line, work), blocks), -1)
        code = owner_ref[h] * work + lax.rem(line, work)
        codes = jnp.where(rows == device, code, codes)
    tags_ref[block] = codes
    lanes = lax.broadcasted_iota(jnp.int32, (1, 64), 1)
    for h in range(home):
        for side, start in enumerate((0, 448)):
            live = (((lanes + start) * 167) & 511) < counts_ref[h]
            values = features_ref[h, :, start : start + 64].astype(F32)
            layers_ref[1, h, :, side * 64 : side * 64 + 64] = jnp.where(live, values, 0.0).astype(
                BF16
            )
    outs = adjoint_ref.shape[1] // 2
    for s in range(work):
        row = adjoint_ref[s].astype(F32)
        adjoints[region, s] = jnp.concatenate([row[:outs], row[outs:]], axis=1).astype(BF16)
    greet(region, block, regions, blocks)

    before = lax.rem(block + blocks - 1, blocks)
    after = lax.rem(block + 1, blocks)
    sends = []
    for k in range(1, regions):
        copy = remote(
            adjoints.at[region],
            adjoints.at[region],
            adj_send.at[k],
            adj_recv.at[k],
            (lax.rem(region + k, regions), block),
        )
        copy.start()
        sends.append(copy)
    for k in range(1, blocks):
        copy = remote(
            tags_ref.at[block],
            tags_ref.at[block],
            tag_send.at[k],
            tag_recv.at[k],
            (region, lax.rem(block + k, blocks)),
        )
        copy.start()
        sends.append(copy)
    for i, (slot, target) in enumerate(((2, before), (0, after))):
        copy = remote(
            layers_ref.at[1], layers_ref.at[slot], lay_send.at[i], lay_recv.at[i], (region, target)
        )
        copy.start()
        sends.append(copy)
    for k in range(1, regions):
        source = lax.rem(region + regions - k, regions)
        remote(
            adjoints.at[source],
            adjoints.at[source],
            adj_send.at[k],
            adj_recv.at[k],
            (source, block),
        ).wait_recv()
    for k in range(1, blocks):
        source = lax.rem(block + blocks - k, blocks)
        remote(
            tags_ref.at[source],
            tags_ref.at[source],
            tag_send.at[k],
            tag_recv.at[k],
            (region, source),
        ).wait_recv()
        code = tags_ref[source, pl.ds(block, 1), :]

        def add(j, total, code=code):
            chosen = jnp.where(code == j, 1.0, 0.0)
            return total + chosen * adjoints[lax.div(j, work), lax.rem(j, work)].astype(F32)

        total = lax.fori_loop(
            0, regions * work, add, jnp.zeros(cotangent_ref.shape[1:], F32)
        )
        outgoing[source] = total.astype(BF16)
        copy = remote(
            outgoing.at[source],
            cotangent_ref.at[block],
            cot_send.at[blocks - k],
            cot_recv.at[blocks - k],
            (region, source),
        )
        copy.start()
        sends.append(copy)
    code = tags_ref[block, pl.ds(block, 1), :]

    def add_own(j, total):
        chosen = jnp.where(code == j, 1.0, 0.0)
        return total + chosen * adjoints[lax.div(j, work), lax.rem(j, work)].astype(F32)

    cotangent_ref[block] = lax.fori_loop(
        0, regions * work, add_own, jnp.zeros(cotangent_ref.shape[1:], F32)
    ).astype(BF16)
    for i, (slot, target) in enumerate(((2, after), (0, before))):
        remote(
            layers_ref.at[1], layers_ref.at[slot], lay_send.at[i], lay_recv.at[i], (region, target)
        ).wait_recv()
    for k in range(1, blocks):
        source = lax.rem(block + blocks - k, blocks)
        remote(
            outgoing.at[source],
            cotangent_ref.at[source],
            cot_send.at[k],
            cot_recv.at[k],
            (region, source),
        ).wait_recv()
    for copy in sends:
        copy.wait_send()


def column(ea, eb, ec):
    t = 9 * (ea + 1) + 3 * (eb + 1) + (ec + 1)
    return t if t < 13 else t - 1


def compute_kernel(
    blocks,
    counts_ref,
    rebalance_ref,
    neighbors_ref,
    features_ref,
    layers_ref,
    cotangent_ref,
    weight_ref,
    bias_ref,
    pooled_ref,
    grad_ref,
    bias_grad_ref,
    cubes,
    slabs,
    stacked,
    total,
):
    home, channels = features_ref.shape[0], features_ref.shape[1]
    work = home // 2
    first = (lax.axis_index("region") * blocks + lax.axis_index("block")) * home
    voxel = lax.broadcasted_iota(jnp.int32, (1, 512), 1)
    hashed = (voxel * 167) & 511
    for h in range(home):
        cubes[h] = jnp.where(hashed < counts_ref[h], features_ref[h].astype(F32), 0.0)
        for d in range(3):
            slabs[d * home + h] = layers_ref[d, h].astype(F32)
    cubes[home] = jnp.zeros(cubes.shape[1:], F32)
    slabs[3 * home] = jnp.zeros(slabs.shape[1:], F32)
    total[...] = jnp.zeros_like(total)
    bias_grad_ref[...] = jnp.zeros_like(bias_grad_ref)
    pooled_ref[...] = jnp.zeros_like(pooled_ref)

    v = lax.broadcasted_iota(jnp.int32, (512, 64), 0)
    cell = ((v >> 7) * 4 + ((v >> 4) & 3)) * 4 + ((v & 7) >> 1)
    table = jnp.where(
        cell == lax.broadcasted_iota(jnp.int32, (512, 64), 1), 0.125, 0.0
    ).astype(BF16)
    lane = lax.broadcasted_iota(jnp.int32, (1, 640), 1)
    b_at, c_at = (lane >> 3) & 7, lane & 7
    half = lax.broadcasted_iota(jnp.int32, (1, 128), 1) < 64

    def shifted(x, offset):
        return pltpu.roll(x, (-offset) % 640, 1)

    def one_block(g, carry):
        def slab(ea, fb, fc):
            target = neighbors_ref[g, column(ea, fb, fc)]
            return slabs[jnp.where(target >= 0, target - (first - home), 3 * home)]

        def extended(fb, fc):
            if (fb, fc) == (0, 0):
                middle = cubes[g]
            else:
                target = neighbors_ref[g, column(0, fb, fc)]
                middle = cubes[jnp.where(target >= 0, target - first, home)]
            ends = jnp.where(half, slab(1, fb, fc), slab(-1, fb, fc))
            return jnp.concatenate([middle, ends], axis=1)

        for ec in (-1, 0, 1):
            along = {}
            for fb in (-1, 0, 1):
                if ec == 0:
                    along[fb] = extended(fb, 0)
                else:
                    out = (c_at + ec) != ((c_at + ec) & 7)
                    along[fb] = jnp.where(
                        out,
                        shifted(extended(fb, ec), -7 * ec),
                        shifted(extended(fb, 0), ec),
                    )
            for eb in (-1, 0, 1):
                if eb == 0:
                    plane = along[0]
                else:
                    out = (b_at + eb) != ((b_at + eb) & 7)
                    plane = jnp.where(
                        out, shifted(along[eb], -56 * eb), shifted(along[0], 8 * eb)
                    )
                for ea in (-1, 0, 1):
                    tap = 9 * (ea + 1) + 3 * (eb + 1) + (ec + 1)
                    moved = plane if ea == 0 else shifted(plane, 64 * ea)
                    stacked[tap * channels : (tap + 1) * channels, :] = moved[:, :512].astype(BF16)

        preact = (
            lax.dot_general(
                weight_ref[...],
                stacked[...],
                (((0,), (0,)), ((), ())),
                preferred_element_type=F32,
            )
            + bias_ref[...]
        )
        live = hashed < counts_ref[g]
        gate = jax.nn.sigmoid(preact)
        active = jnp.where(live, preact * gate, 0.0)
        high = active.astype(BF16)
        low = (active - high.astype(F32)).astype(BF16)
        pooled = jnp.dot(high, table, preferred_element_type=F32) + jnp.dot(
            low, table, preferred_element_type=F32
        )
        line = rebalance_ref[g]
        device = jnp.where(line >= 0, lax.rem(lax.div(line, work), blocks), blocks)
        middle = pooled.shape[0] // 2
        pooled_ref[device] = jnp.concatenate([pooled[:middle], pooled[middle:]], axis=1).astype(
            BF16
        )
        row = cotangent_ref[jnp.minimum(device, blocks - 1)].astype(F32)
        width = row.shape[1] // 2
        row = jnp.concatenate([row[:, :width], row[:, width:]], axis=0).astype(BF16)
        spread = lax.dot_general(
            row,
            table,
            (((1,), (1,)), ((), ())),
            preferred_element_type=F32,
        )
        grad = jnp.where(live, spread * gate * (1.0 + preact * (1.0 - gate)), 0.0)
        grad_high = grad.astype(BF16)
        grad_low = (grad - grad_high.astype(F32)).astype(BF16)
        total[...] += lax.dot_general(
            stacked[...], grad_high, (((1,), (1,)), ((), ())), preferred_element_type=F32
        )
        ones = jnp.ones((8, 512), BF16)
        for part in (grad_high, grad_low):
            bias_grad_ref[...] += lax.dot_general(
                ones, part, (((1,), (1,)), ((), ())), preferred_element_type=F32
            )
        return carry

    lax.fori_loop(0, home, one_block, 0)
    used = total.shape[0]
    grad_ref[:used, :] = total[...]
    if grad_ref.shape[0] > used:
        grad_ref[used:, :] = jnp.zeros((grad_ref.shape[0] - used, grad_ref.shape[1]), F32)


def reduce_kernel(
    regions,
    blocks,
    shard,
    pooled_in,
    tags_ref,
    grad_ref,
    bias_ref,
    pooled_ref,
    weight_out,
    bias_out,
    pooled_got,
    pooled_sel,
    pooled_end,
    pair_got,
    pair_sum,
    grad_got,
    grad_part,
    grad_slice,
    grad_full,
    grad_all,
    bias_got,
    bias_part,
    p_send,
    p_recv,
    q_send,
    q_recv,
    e_send,
    e_recv,
    f_send,
    f_recv,
    g_send,
    g_recv,
    h_send,
    h_recv,
    d_send,
    d_recv,
    a_send,
    a_recv,
    b_send,
    b_recv,
    c_send,
    c_recv,
):
    region, block = lax.axis_index("region"), lax.axis_index("block")
    work = pooled_ref.shape[0]
    greet(region, block, regions, blocks)
    sends = []

    def start(*args):
        copy = remote(*args)
        copy.start()
        sends.append(copy)

    def across(k):
        return (region, lax.rem(block + k, blocks))

    def along(k):
        return (lax.rem(region + k, regions), block)

    core, chip, chips = lax.rem(block, 2), lax.div(block, 2), blocks // 2
    sibling = (region, block + 1 - 2 * core)

    def part(side, j):
        index = side * chips + lax.rem(chip + j, chips)
        return pl.ds(pl.multiple_of(index * shard, 16), shard)

    def other_chip(j):
        return (region, 2 * lax.rem(chip + j, chips) + core)

    for k in range(1, blocks):
        peer = lax.rem(block + k, blocks)
        start(pooled_in.at[peer], pooled_got.at[k], p_send.at[k], p_recv.at[k], across(k))
        start(bias_ref, bias_got.at[k], b_send.at[k], b_recv.at[k], across(k))
    for j in (*range(1, chips), 0):
        start(
            grad_ref.at[part(1 - core, j)], pair_got.at[j], e_send.at[j], e_recv.at[j], sibling
        )
    pooled_got[0] = pooled_in[block]
    for j in (*range(1, chips), 0):
        remote(
            grad_ref.at[part(1 - core, j)], pair_got.at[j], e_send.at[j], e_recv.at[j], sibling
        ).wait_recv()
        grad_sum = grad_ref[part(core, j), :] + pair_got[j]
        if j > 0:
            pair_sum[j] = grad_sum.astype(BF16)
            start(pair_sum.at[j], grad_got.at[j], g_send.at[j], g_recv.at[j], other_chip(j))
    for k in range(1, blocks):
        remote(
            pooled_in.at[0], pooled_got.at[k], p_send.at[k], p_recv.at[k], across(k)
        ).wait_recv()

    def select(j, carry):
        def add(k, total):
            code = tags_ref[lax.rem(block + blocks - k, blocks), pl.ds(block, 1), :]
            return total + jnp.where(code == j, 1.0, 0.0) * pooled_got[k].astype(F32)

        total = lax.fori_loop(0, blocks, add, jnp.zeros(pooled_got.shape[1:], F32))
        pooled_sel[lax.div(j, work), lax.rem(j, work)] = total.astype(BF16)
        return carry

    lax.fori_loop(0, regions * work, select, 0)
    for k in range(1, regions):
        peer = lax.rem(region + k, regions)
        start(pooled_sel.at[peer], pooled_end.at[k], q_send.at[k], q_recv.at[k], along(k))
    bias_sum = bias_ref[...]
    for k in range(1, blocks):
        remote(bias_ref, bias_got.at[k], b_send.at[k], b_recv.at[k], across(k)).wait_recv()
        bias_sum = bias_sum + bias_got[k]
    bias_part[region] = bias_sum
    for k in range(1, regions):
        start(
            bias_part.at[region], bias_part.at[region], c_send.at[k], c_recv.at[k], along(k)
        )

    for j in range(1, chips):
        remote(
            pair_sum.at[j], grad_got.at[j], g_send.at[j], g_recv.at[j], other_chip(j)
        ).wait_recv()
        grad_sum = grad_sum + grad_got[j].astype(F32)
    grad_part[...] = grad_sum.reshape(grad_part.shape)
    for k in range(1, regions):
        peer = lax.rem(region + k, regions)
        start(grad_part.at[peer], grad_slice.at[k], h_send.at[k], h_recv.at[k], along(k))
    for k in range(1, regions):
        remote(
            grad_part.at[0], grad_slice.at[k], h_send.at[k], h_recv.at[k], along(k)
        ).wait_recv()
    grad_sum = grad_part[region]
    for k in range(1, regions):
        grad_sum = grad_sum + grad_slice[k]
    grad_full[region] = grad_sum
    for k in range(1, regions):
        start(
            grad_full.at[region], grad_full.at[region], d_send.at[k], d_recv.at[k], along(k)
        )
    for k in range(1, regions):
        source = lax.rem(region + regions - k, regions)
        remote(
            grad_full.at[source], grad_full.at[source], d_send.at[k], d_recv.at[k], along(k)
        ).wait_recv()
    grad_sum = grad_full[...].reshape(shard, -1)
    own = grad_all.at[core, chip]
    own[...] = grad_sum.astype(BF16)
    for j in range(1, chips):
        start(own, own, a_send.at[j], a_recv.at[j], other_chip(j))
    start(own, own, f_send.at[0], f_recv.at[0], sibling)
    for j in range(1, chips):
        slot = grad_all.at[core, lax.rem(chip + chips - j, chips)]
        remote(slot, slot, a_send.at[j], a_recv.at[j], other_chip(j)).wait_recv()
        start(slot, slot, f_send.at[j], f_recv.at[j], sibling)

    for k in range(1, regions):
        source = lax.rem(region + regions - k, regions)
        remote(
            bias_part.at[source], bias_part.at[source], c_send.at[k], c_recv.at[k], along(k)
        ).wait_recv()
        remote(
            pooled_sel.at[0], pooled_end.at[k], q_send.at[k], q_recv.at[k], along(k)
        ).wait_recv()
    bias_sum = bias_part[0]
    for r in range(1, regions):
        bias_sum = bias_sum + bias_part[r]
    bias_out[...] = bias_sum
    for s in range(work):
        rows = pooled_sel[region, s].astype(F32)
        for k in range(1, regions):
            rows = rows + pooled_end[k, s].astype(F32)
        width = rows.shape[1] // 2
        pooled_ref[s] = jnp.concatenate([rows[:, :width], rows[:, width:]], axis=0).astype(BF16)

    for j in range(chips):
        slot = grad_all.at[1 - core, lax.rem(chip + chips - j, chips)]
        remote(slot, slot, f_send.at[j], f_recv.at[j], sibling).wait_recv()
    rows_total = weight_out.shape[0]
    for w in range(blocks):
        low, high = w * shard, min((w + 1) * shard, rows_total)
        if low < high:
            weight_out[low:high, :] = grad_all[w // chips, w % chips, : high - low, :].astype(F32)
    for copy in sends:
        copy.wait_send()


def per_device(
    features,
    counts,
    rebalance,
    neighbors,
    coarse_owner,
    conv_weight,
    convolution_bias_vector,
    merged_adjoint,
):
    home, channels = features.shape[0], features.shape[1]
    taps, _, outs = conv_weight.shape
    work = home // 2
    regions, blocks = lax.axis_size("region"), lax.axis_size("block")
    cells = merged_adjoint.shape[1] // outs
    rows = taps * channels
    dense = (outs // 2, 2 * cells)
    chips = blocks // 2
    unit = math.lcm(16, 8 * regions)
    shard = -(-rows // (blocks * unit)) * unit
    vmem = pl.BlockSpec(memory_space=pltpu.VMEM)
    smem = pl.BlockSpec(memory_space=pltpu.SMEM)
    dma = pltpu.SemaphoreType.DMA
    shape = jax.ShapeDtypeStruct

    layers, cotangent, tags = pl.pallas_call(
        functools.partial(exchange_kernel, regions, blocks),
        out_shape=(
            shape((3, home, channels, 128), BF16),
            shape((blocks,) + dense, BF16),
            shape((blocks, blocks, 128), jnp.int32),
        ),
        in_specs=[smem, smem, smem, vmem, vmem],
        out_specs=(vmem, vmem, vmem),
        scratch_shapes=[
            pltpu.VMEM((regions, work) + dense, BF16),
            pltpu.VMEM((blocks,) + dense, BF16),
            dma((regions,)),
            dma((regions,)),
            dma((blocks,)),
            dma((blocks,)),
            dma((2,)),
            dma((2,)),
            dma((blocks,)),
            dma((blocks,)),
        ],
        compiler_params=pltpu.CompilerParams(
            collective_id=0, has_side_effects=True, vmem_limit_bytes=VMEM_LIMIT
        ),
        name="exchange",
    )(counts, rebalance, coarse_owner, features, merged_adjoint.reshape(work, outs, cells))

    pooled_send, grad_send, bias_send = pl.pallas_call(
        functools.partial(compute_kernel, blocks),
        out_shape=(
            shape((blocks + 1,) + dense, BF16),
            shape((blocks * shard, outs), F32),
            shape((8, outs), F32),
        ),
        in_specs=[smem, smem, smem, vmem, vmem, vmem, vmem, vmem],
        out_specs=(vmem, vmem, vmem),
        scratch_shapes=[
            pltpu.VMEM((home + 1, channels, 512), F32),
            pltpu.VMEM((3 * home + 1, channels, 128), F32),
            pltpu.VMEM((rows, 512), BF16),
            pltpu.VMEM((rows, outs), F32),
        ],
        compiler_params=pltpu.CompilerParams(vmem_limit_bytes=VMEM_LIMIT),
        name="convolve",
    )(
        counts,
        rebalance,
        neighbors,
        features,
        layers,
        cotangent,
        conv_weight.reshape(rows, outs),
        convolution_bias_vector.reshape(outs, 1),
    )

    pooled, weight_total, bias_total = pl.pallas_call(
        functools.partial(reduce_kernel, regions, blocks, shard),
        out_shape=(
            shape((work, outs, cells), BF16),
            shape((rows, outs), F32),
            shape((8, outs), F32),
        ),
        in_specs=[vmem] * 4,
        out_specs=(vmem, vmem, vmem),
        scratch_shapes=[
            pltpu.VMEM((blocks,) + dense, BF16),
            pltpu.VMEM((regions, work) + dense, BF16),
            pltpu.VMEM((regions, work) + dense, BF16),
            pltpu.VMEM((chips, shard, outs), F32),
            pltpu.VMEM((chips, shard, outs), BF16),
            pltpu.VMEM((chips, shard, outs), BF16),
            pltpu.VMEM((regions, shard // regions, outs), F32),
            pltpu.VMEM((regions, shard // regions, outs), F32),
            pltpu.VMEM((regions, shard // regions, outs), F32),
            pltpu.VMEM((2, chips, shard, outs), BF16),
            pltpu.VMEM((blocks, 8, outs), F32),
            pltpu.VMEM((regions, 8, outs), F32),
            dma((blocks,)),
            dma((blocks,)),
            dma((regions,)),
            dma((regions,)),
            dma((chips,)),
            dma((chips,)),
            dma((chips,)),
            dma((chips,)),
            dma((chips,)),
            dma((chips,)),
            dma((regions,)),
            dma((regions,)),
            dma((regions,)),
            dma((regions,)),
            dma((chips,)),
            dma((chips,)),
            dma((blocks,)),
            dma((blocks,)),
            dma((regions,)),
            dma((regions,)),
        ],
        compiler_params=pltpu.CompilerParams(
            collective_id=1, has_side_effects=True, vmem_limit_bytes=VMEM_LIMIT
        ),
        name="reduce",
    )(pooled_send, tags, grad_send, bias_send)
    return (
        pooled.reshape(work, outs * cells),
        weight_total.reshape(taps, channels, outs),
        bias_total[0],
    )


def solution(mesh):
    in_specs = (
        P(("region", "block"), None, None),
        P(("region", "block")),
        P(("region", "block")),
        P(("region", "block"), None),
        P(("region", "block")),
        P(),
        P(),
        P(("region", "block"), None),
    )
    out_specs = (P(("region", "block"), None), P(), P())
    return jax.shard_map(
        per_device, mesh=mesh, in_specs=in_specs, out_specs=out_specs, check_vma=False
    )
```

profile of v0, /device:TPU:1, one launch (start us, length us, event | category | flops | bytes accessed | tf_op | source)
XLA Modules:
  0.0 56.2 jit_solution(6171876193476986282)
XLA Ops:
  0.6 0.0 copy-start.8
  0.6 0.6 %copy-done.8 = f32[128]{0:T(128)S(1)} copy-done((f32[128]{0:T(128)S(1)}, f32[128]{0:T(128)}, u32[]{:S(2)}) %copy-start.8) | copy-done | bytes 536
  1.3 0.0 copy-start.7
  1.3 0.1 copy.12.bias_ref
  1.4 0.6 %copy-done.7 = bf16[2,8192]{1,0:T(2,128)(2,1)S(1)} copy-done((bf16[2,8192]{1,0:T(2,128)(2,1)S(1)}, bf16[2,8192]{1,0:T(2,128)(2,1)}, u32[]{:S(2)}) %copy-start.7) | copy-done | bytes 32792
  2.0 0.0 copy-start.3
  2.0 0.0 copy-start.4
  2.0 0.0 copy-start.6
  2.1 0.1 reshape.21.adjoint_ref
  2.2 0.5 copy-done.3
  2.7 0.0 copy-done.4
  2.7 0.0 copy-done.6
  2.7 0.0 copy-start
  2.7 0.9 %copy-done = bf16[4,64,512]{2,1,0:T(8,128)(2,1)S(1)} copy-done((bf16[4,64,512]{2,1,0:T(8,128)(2,1)S(1)}, bf16[4,64,512]{2,1,0:T(8,128)(2,1)}, u32[]{:S(2)}) %copy-start) | copy-done | bytes 262168
  3.7 13.6 %exchange.1 = (bf16[3,4,64,128]{3,2,1,0:T(8,128)(2,1)S(1)}, bf16[8,64,128]{2,1,0:T(8,128)(2,1)S(1)}, s32[8,8,128]{2,1,0:T(8,128)S(1)}) custom-call(s32[4]{0:T(128)S(1)} %copy-done.3, s32[4]{0:T(128)S(1)} %copy-done.4, s32[4]{0:T(128)S(1)} %copy-done.6, bf16[4,64,512]{2,1,0:T(8,128)(2,1)S(1)} %copy-done, bf16[2,128,64]{2,1,0:T(8,128)(2,1)S(1)} %reshape.21.adjoint_ref), custom_call_target="tpu_custom_call" | custom-call | tf_op jit(solution)/shard_map/exchange/pallas_call | solution.py:529
  17.3 0.0 copy-start.5
  17.3 0.0 copy-done.1
  17.4 0.7 %copy-done.5 = s32[4,26]{1,0:T(4,128)S(1)} copy-done((s32[4,26]{1,0:T(4,128)S(1)}, s32[4,26]{1,0:T(4,128)}, u32[]{:S(2)}) %copy-start.5) | copy-done | bytes 440
  18.0 1.0 %copy-done.2 = bf16[27,64,128]{2,1,0:T(8,128)(2,1)S(1)} copy-done((bf16[27,64,128]{2,1,0:T(8,128)(2,1)S(1)}, bf16[27,64,128]{2,1,0:T(8,128)(2,1)}, u32[]{:S(2)}) %copy-start.2) | copy-done | bytes 442392
  19.0 9.3 %convolve.1 = (bf16[9,64,128]{2,1,0:T(8,128)(2,1)S(1)}, f32[1792,128]{1,0:T(8,128)S(1)}, f32[8,128]{1,0:T(8,128)S(1)}) custom-call(s32[4]{0:T(128)S(1)} %copy-done.3, s32[4]{0:T(128)S(1)} %copy-done.4, s32[4,26]{1,0:T(4,128)S(1)} %copy-done.5, bf16[4,64,512]{2,1,0:T(8,128)(2,1)S(1)} %copy-done.1, bf16[3,4,64,128]{3,2,1,0:T(8,128)(2,1)S(1)} %get-tuple-element.12.layers_ref, ...), custom_call_target="tpu_custom_call" | custom-call | tf_op jit(solution)/shard_map/convolve/pallas_call | solution.py:556
  28.3 25.8 %reduce.1 = (bf16[2,128,64]{2,1,0:T(8,128)(2,1)S(1)}, f32[1728,128]{1,0:T(8,128)S(1)}, f32[8,128]{1,0:T(8,128)S(1)}) custom-call(bf16[9,64,128]{2,1,0:T(8,128)(2,1)S(1)} %get-tuple-element.14.pooled_in, s32[8,8,128]{2,1,0:T(8,128)S(1)} %get-tuple-element.15.tags_ref, f32[1792,128]{1,0:T(8,128)S(1)} %get-tuple-element.16.grad_ref, ...), custom_call_target="tpu_custom_call" | custom-call | tf_op jit(solution)/shard_map/reduce/pallas_call | solution.py:584
  54.1 0.7 %reshape.24 = bf16[2,8192]{1,0:T(2,128)(2,1)} reshape(bf16[2,128,64]{2,1,0:T(8,128)(2,1)S(1)} %get-tuple-element.18) | data formatting | bytes 65536 | tf_op jit(solution)/shard_map/reshape | solution.py:633
  54.8 0.5 slice_bitcast_fusion
  55.3 0.9 %copy.14 = f32[27,64,128]{2,1,0:T(8,128)} copy(f32[27,64,128]{2,1,0:T(8,128)S(1)} %bitcast.5) | data formatting | bytes 1769472
  (2 shorter events, 0.0 us)
Async XLA Ops:
  0.6 0.7 %copy-start.8 = (f32[128]{0:T(128)S(1)}, f32[128]{0:T(128)}, u32[]{:S(2)}) copy-start(f32[128]{0:T(128)} %param.14) | copy-start | bytes 1540
  1.3 0.8 %copy-start.7 = (bf16[2,8192]{1,0:T(2,128)(2,1)S(1)}, bf16[2,8192]{1,0:T(2,128)(2,1)}, u32[]{:S(2)}) copy-start(bf16[2,8192]{1,0:T(2,128)(2,1)} %param.15) | copy-start | bytes 98308
  2.0 0.7 %copy-start.3 = (s32[4]{0:T(128)S(1)}, s32[4]{0:T(128)}, u32[]{:S(2)}) copy-start(s32[4]{0:T(128)} %counts_ref.3) | copy-start | bytes 52
  2.0 0.7 %copy-start.4 = (s32[4]{0:T(128)S(1)}, s32[4]{0:T(128)}, u32[]{:S(2)}) copy-start(s32[4]{0:T(128)} %rebalance_ref.3) | copy-start | bytes 52
  2.0 0.7 %copy-start.6 = (s32[4]{0:T(128)S(1)}, s32[4]{0:T(128)}, u32[]{:S(2)}) copy-start(s32[4]{0:T(128)} %owner_ref.1) | copy-start | bytes 52
  2.7 0.9 %copy-start = (bf16[4,64,512]{2,1,0:T(8,128)(2,1)S(1)}, bf16[4,64,512]{2,1,0:T(8,128)(2,1)}, u32[]{:S(2)}) copy-start(bf16[4,64,512]{2,1,0:T(8,128)(2,1)} %features_ref.3) | copy-start | bytes 786436
  3.7 13.7 %copy-start.1 = (bf16[4,64,512]{2,1,0:T(8,128)(2,1)S(1)}, bf16[4,64,512]{2,1,0:T(8,128)(2,1)}, u32[]{:S(2)}) copy-start(bf16[4,64,512]{2,1,0:T(8,128)(2,1)} %features_ref.3) | copy-start | bytes 786436
  17.3 0.7 %copy-start.5 = (s32[4,26]{1,0:T(4,128)S(1)}, s32[4,26]{1,0:T(4,128)}, u32[]{:S(2)}) copy-start(s32[4,26]{1,0:T(4,128)} %neighbors_ref.1) | copy-start | bytes 1252
  18.0 1.0 %copy-start.2 = (bf16[27,64,128]{2,1,0:T(8,128)(2,1)S(1)}, bf16[27,64,128]{2,1,0:T(8,128)(2,1)}, u32[]{:S(2)}) copy-start(bf16[27,64,128]{2,1,0:T(8,128)(2,1)} %param.13) | copy-start | bytes 1327108
where the time goes:
time: 56.5 us; the launch traced here: 56.2 us
  Pallas kernels  48.6 us (86%)
  local copies, waits for them, and re-layouts  6.87 us (12%)
  between operations  0.69 us (1%)
    pallas_call x1, Pallas kernels, per_device(): pl.pallas_call(functools.partial(reduce_kernel, regions, blocks, shard),...  25.8 us
    pallas_call x1, Pallas kernels, per_device(): pl.pallas_call(functools.partial(exchange_kernel, regions, blocks), out_s...  13.6 us
    pallas_call x1, Pallas kernels, per_device(): pl.pallas_call(functools.partial(compute_kernel, blocks), out_shape=(shap...  9.26 us
    unnamed x19, local copies, waits for them, and re-layouts  5.41 us

commit v1 on v0

--- a/solution.py
+++ b/solution.py
@@ -48,9 +48,12 @@
     adjoint_ref,
     layers_ref,
     cotangent_ref,
+    mine_ref,
     tags_ref,
+    codes_ref,
     adjoints,
     outgoing,
+    code_sem,
     adj_send,
     adj_recv,
     tag_send,
@@ -82,7 +85,7 @@
     outs = adjoint_ref.shape[1] // 2
     for s in range(work):
         row = adjoint_ref[s].astype(F32)
-        adjoints[region, s] = jnp.concatenate([row[:outs], row[outs:]], axis=1).astype(BF16)
+        adjoints[region * work + s] = jnp.concatenate([row[:outs], row[outs:]], axis=1).astype(BF16)
     greet(region, block, regions, blocks)
 
     before = lax.rem(block + blocks - 1, blocks)
@@ -90,8 +93,8 @@
     sends = []
     for k in range(1, regions):
         copy = remote(
-            adjoints.at[region],
-            adjoints.at[region],
+            adjoints.at[pl.ds(region * work, work)],
+            adjoints.at[pl.ds(region * work, work)],
             adj_send.at[k],
             adj_recv.at[k],
             (lax.rem(region + k, regions), block),
@@ -114,15 +117,6 @@
         )
         copy.start()
         sends.append(copy)
-    for k in range(1, regions):
-        source = lax.rem(region + regions - k, regions)
-        remote(
-            adjoints.at[source],
-            adjoints.at[source],
-            adj_send.at[k],
-            adj_recv.at[k],
-            (source, block),
-        ).wait_recv()
     for k in range(1, blocks):
         source = lax.rem(block + blocks - k, blocks)
         remote(
@@ -132,16 +126,23 @@
             tag_recv.at[k],
             (region, source),
         ).wait_recv()
-        code = tags_ref[source, pl.ds(block, 1), :]
-
-        def add(j, total, code=code):
-            chosen = jnp.where(code == j, 1.0, 0.0)
-            return total + chosen * adjoints[lax.div(j, work), lax.rem(j, work)].astype(F32)
-
-        total = lax.fori_loop(
-            0, regions * work, add, jnp.zeros(cotangent_ref.shape[1:], F32)
-        )
-        outgoing[source] = total.astype(BF16)
+        mine_ref[pl.ds(source, 1), :] = tags_ref[source, pl.ds(block, 1), :]
+    mine_ref[pl.ds(block, 1), :] = tags_ref[block, pl.ds(block, 1), :]
+    codes_copy = pltpu.make_async_copy(mine_ref, codes_ref, code_sem)
+    codes_copy.start()
+    codes_copy.wait()
+    for k in range(1, regions):
+        source = lax.rem(region + regions - k, regions)
+        remote(
+            adjoints.at[pl.ds(source * work, work)],
+            adjoints.at[pl.ds(source * work, work)],
+            adj_send.at[k],
+            adj_recv.at[k],
+            (source, block),
+        ).wait_recv()
+    for k in range(1, blocks):
+        source = lax.rem(block + blocks - k, blocks)
+        outgoing[source] = adjoints[jnp.maximum(codes_ref[source, 0], 0)]
         copy = remote(
             outgoing.at[source],
             cotangent_ref.at[block],
@@ -151,15 +152,7 @@
         )
         copy.start()
         sends.append(copy)
-    code = tags_ref[block, pl.ds(block, 1), :]
-
-    def add_own(j, total):
-        chosen = jnp.where(code == j, 1.0, 0.0)
-        return total + chosen * adjoints[lax.div(j, work), lax.rem(j, work)].astype(F32)
-
-    cotangent_ref[block] = lax.fori_loop(
-        0, regions * work, add_own, jnp.zeros(cotangent_ref.shape[1:], F32)
-    ).astype(BF16)
+    cotangent_ref[block] = adjoints[jnp.maximum(codes_ref[block, 0], 0)]
     for i, (slot, target) in enumerate(((2, after), (0, before))):
         remote(
             layers_ref.at[1], layers_ref.at[slot], lay_send.at[i], lay_recv.at[i], (region, target)
@@ -323,7 +316,7 @@
     blocks,
     shard,
     pooled_in,
-    tags_ref,
+    codes_ref,
     grad_ref,
     bias_ref,
     pooled_ref,
@@ -411,11 +404,12 @@
         ).wait_recv()
 
     def select(j, carry):
-        def add(k, total):
-            code = tags_ref[lax.rem(block + blocks - k, blocks), pl.ds(block, 1), :]
-            return total + jnp.where(code == j, 1.0, 0.0) * pooled_got[k].astype(F32)
-
-        total = lax.fori_loop(0, blocks, add, jnp.zeros(pooled_got.shape[1:], F32))
+        slot, found = 0, 0.0
+        for k in range(blocks):
+            hit = codes_ref[lax.rem(block + blocks - k, blocks), 0] == j
+            slot = jnp.where(hit, k, slot)
+            found = jnp.where(hit, 1.0, found)
+        total = pooled_got[slot].astype(F32) * found
         pooled_sel[lax.div(j, work), lax.rem(j, work)] = total.astype(BF16)
         return carry
 
@@ -526,18 +520,21 @@
     dma = pltpu.SemaphoreType.DMA
     shape = jax.ShapeDtypeStruct
 
-    layers, cotangent, tags = pl.pallas_call(
+    layers, cotangent, codes = pl.pallas_call(
         functools.partial(exchange_kernel, regions, blocks),
         out_shape=(
             shape((3, home, channels, 128), BF16),
             shape((blocks,) + dense, BF16),
-            shape((blocks, blocks, 128), jnp.int32),
+            shape((blocks, 128), jnp.int32),
         ),
         in_specs=[smem, smem, smem, vmem, vmem],
         out_specs=(vmem, vmem, vmem),
         scratch_shapes=[
-            pltpu.VMEM((regions, work) + dense, BF16),
+            pltpu.VMEM((blocks, blocks, 128), jnp.int32),
+            pltpu.SMEM((blocks, 128), jnp.int32),
+            pltpu.VMEM((regions * work,) + dense, BF16),
             pltpu.VMEM((blocks,) + dense, BF16),
+            dma,
             dma((regions,)),
             dma((regions,)),
             dma((blocks,)),
@@ -588,7 +585,7 @@
             shape((rows, outs), F32),
             shape((8, outs), F32),
         ),
-        in_specs=[vmem] * 4,
+        in_specs=[vmem, smem, vmem, vmem],
         out_specs=(vmem, vmem, vmem),
         scratch_shapes=[
             pltpu.VMEM((blocks,) + dense, BF16),
@@ -628,7 +625,7 @@
             collective_id=1, has_side_effects=True, vmem_limit_bytes=VMEM_LIMIT
         ),
         name="reduce",
-    )(pooled_send, tags, grad_send, bias_send)
+    )(pooled_send, codes, grad_send, bias_send)
     return (
         pooled.reshape(work, outs * cells),
         weight_total.reshape(taps, channels, outs),

time: 56.5 us -> 56.4 us (level)
  no operation moved by 1% of the time
where the time goes in v1:
time: 56.4 us; the launch traced here: 56.1 us
  Pallas kernels  48.6 us (86%)
  local copies, waits for them, and re-layouts  6.87 us (12%)
  between operations  0.69 us (1%)
    pallas_call x1, Pallas kernels, per_device(): pl.pallas_call(functools.partial(reduce_kernel, regions, blocks, shard),...  25.7 us
    pallas_call x1, Pallas kernels, per_device(): pl.pallas_call(functools.partial(exchange_kernel, regions, blocks), out_s...  13.6 us
    pallas_call x1, Pallas kernels, per_device(): pl.pallas_call(functools.partial(compute_kernel, blocks), out_shape=(shap...  9.26 us
    unnamed x19, local copies, waits for them, and re-layouts  5.41 us

profile of v1, /device:TPU:1, one launch (start us, length us, event | category | flops | bytes accessed | tf_op | source)
XLA Modules:
  0.0 56.1 jit_solution(7755118243830231015)
XLA Ops:
  0.6 0.0 copy-start.8
  0.6 0.6 %copy-done.8 = f32[128]{0:T(128)S(1)} copy-done((f32[128]{0:T(128)S(1)}, f32[128]{0:T(128)}, u32[]{:S(2)}) %copy-start.8) | copy-done | bytes 536
  1.3 0.1 copy.12.bias_ref
  1.4 0.6 %copy-done.7 = bf16[2,8192]{1,0:T(2,128)(2,1)S(1)} copy-done((bf16[2,8192]{1,0:T(2,128)(2,1)S(1)}, bf16[2,8192]{1,0:T(2,128)(2,1)}, u32[]{:S(2)}) %copy-start.7) | copy-done | bytes 32792
  2.0 0.0 copy-start.3
  2.0 0.0 copy-start.4
  2.0 0.0 copy-start.6
  2.1 0.1 reshape.21.adjoint_ref
  2.2 0.5 copy-done.3
  2.7 0.0 copy-done.4
  2.7 0.0 copy-done.6
  2.7 0.0 copy-start
  2.7 0.9 %copy-done = bf16[4,64,512]{2,1,0:T(8,128)(2,1)S(1)} copy-done((bf16[4,64,512]{2,1,0:T(8,128)(2,1)S(1)}, bf16[4,64,512]{2,1,0:T(8,128)(2,1)}, u32[]{:S(2)}) %copy-start) | copy-done | bytes 262168
  3.7 0.0 copy-start.1
  3.7 13.6 %exchange.1 = (bf16[3,4,64,128]{3,2,1,0:T(8,128)(2,1)S(1)}, bf16[8,64,128]{2,1,0:T(8,128)(2,1)S(1)}, s32[8,128]{1,0:T(8,128)S(1)}) custom-call(s32[4]{0:T(128)S(1)} %copy-done.3, s32[4]{0:T(128)S(1)} %copy-done.4, s32[4]{0:T(128)S(1)} %copy-done.6, bf16[4,64,512]{2,1,0:T(8,128)(2,1)S(1)} %copy-done, bf16[2,128,64]{2,1,0:T(8,128)(2,1)S(1)} %reshape.21.adjoint_ref), custom_call_target="tpu_custom_call" | custom-call | tf_op jit(solution)/shard_map/exchange/pallas_call | solution.py:523
  17.3 0.0 copy-start.5
  17.3 0.0 copy-done.1
  17.3 0.7 %copy-done.5 = s32[4,26]{1,0:T(4,128)S(1)} copy-done((s32[4,26]{1,0:T(4,128)S(1)}, s32[4,26]{1,0:T(4,128)}, u32[]{:S(2)}) %copy-start.5) | copy-done | bytes 440
  18.0 1.0 %copy-done.2 = bf16[27,64,128]{2,1,0:T(8,128)(2,1)S(1)} copy-done((bf16[27,64,128]{2,1,0:T(8,128)(2,1)S(1)}, bf16[27,64,128]{2,1,0:T(8,128)(2,1)}, u32[]{:S(2)}) %copy-start.2) | copy-done | bytes 442392
  19.0 9.3 %convolve.1 = (bf16[9,64,128]{2,1,0:T(8,128)(2,1)S(1)}, f32[1792,128]{1,0:T(8,128)S(1)}, f32[8,128]{1,0:T(8,128)S(1)}) custom-call(s32[4]{0:T(128)S(1)} %copy-done.3, s32[4]{0:T(128)S(1)} %copy-done.4, s32[4,26]{1,0:T(4,128)S(1)} %copy-done.5, bf16[4,64,512]{2,1,0:T(8,128)(2,1)S(1)} %copy-done.1, bf16[3,4,64,128]{3,2,1,0:T(8,128)(2,1)S(1)} %get-tuple-element.12.layers_ref, ...), custom_call_target="tpu_custom_call" | custom-call | tf_op jit(solution)/shard_map/convolve/pallas_call | solution.py:553
  28.2 25.7 %reduce.1 = (bf16[2,128,64]{2,1,0:T(8,128)(2,1)S(1)}, f32[1728,128]{1,0:T(8,128)S(1)}, f32[8,128]{1,0:T(8,128)S(1)}) custom-call(bf16[9,64,128]{2,1,0:T(8,128)(2,1)S(1)} %get-tuple-element.14.pooled_in, s32[8,128]{1,0:T(8,128)S(1)} %get-tuple-element.15.codes_ref, f32[1792,128]{1,0:T(8,128)S(1)} %get-tuple-element.16.grad_ref, ...), custom_call_target="tpu_custom_call" | custom-call | tf_op jit(solution)/shard_map/reduce/pallas_call | solution.py:581
  54.0 0.7 %reshape.24 = bf16[2,8192]{1,0:T(2,128)(2,1)} reshape(bf16[2,128,64]{2,1,0:T(8,128)(2,1)S(1)} %get-tuple-element.18) | data formatting | bytes 65536 | tf_op jit(solution)/shard_map/reshape | solution.py:630
  54.7 0.5 slice_bitcast_fusion
  55.2 0.9 %copy.14 = f32[27,64,128]{2,1,0:T(8,128)} copy(f32[27,64,128]{2,1,0:T(8,128)S(1)} %bitcast.5) | data formatting | bytes 1769472
  (2 shorter events, 0.0 us)
Async XLA Ops:
  0.6 0.7 %copy-start.8 = (f32[128]{0:T(128)S(1)}, f32[128]{0:T(128)}, u32[]{:S(2)}) copy-start(f32[128]{0:T(128)} %param.14) | copy-start | bytes 1540
  1.3 0.8 %copy-start.7 = (bf16[2,8192]{1,0:T(2,128)(2,1)S(1)}, bf16[2,8192]{1,0:T(2,128)(2,1)}, u32[]{:S(2)}) copy-start(bf16[2,8192]{1,0:T(2,128)(2,1)} %param.15) | copy-start | bytes 98308
  2.0 0.7 %copy-start.3 = (s32[4]{0:T(128)S(1)}, s32[4]{0:T(128)}, u32[]{:S(2)}) copy-start(s32[4]{0:T(128)} %counts_ref.3) | copy-start | bytes 52
  2.0 0.7 %copy-start.4 = (s32[4]{0:T(128)S(1)}, s32[4]{0:T(128)}, u32[]{:S(2)}) copy-start(s32[4]{0:T(128)} %rebalance_ref.3) | copy-start | bytes 52
  2.0 0.7 %copy-start.6 = (s32[4]{0:T(128)S(1)}, s32[4]{0:T(128)}, u32[]{:S(2)}) copy-start(s32[4]{0:T(128)} %owner_ref.1) | copy-start | bytes 52
  2.7 0.9 %copy-start = (bf16[4,64,512]{2,1,0:T(8,128)(2,1)S(1)}, bf16[4,64,512]{2,1,0:T(8,128)(2,1)}, u32[]{:S(2)}) copy-start(bf16[4,64,512]{2,1,0:T(8,128)(2,1)} %features_ref.3) | copy-start | bytes 786436
  3.7 13.6 %copy-start.1 = (bf16[4,64,512]{2,1,0:T(8,128)(2,1)S(1)}, bf16[4,64,512]{2,1,0:T(8,128)(2,1)}, u32[]{:S(2)}) copy-start(bf16[4,64,512]{2,1,0:T(8,128)(2,1)} %features_ref.3) | copy-start | bytes 786436
  17.3 0.7 %copy-start.5 = (s32[4,26]{1,0:T(4,128)S(1)}, s32[4,26]{1,0:T(4,128)}, u32[]{:S(2)}) copy-start(s32[4,26]{1,0:T(4,128)} %neighbors_ref.1) | copy-start | bytes 1252
  17.9 1.0 %copy-start.2 = (bf16[27,64,128]{2,1,0:T(8,128)(2,1)S(1)}, bf16[27,64,128]{2,1,0:T(8,128)(2,1)}, u32[]{:S(2)}) copy-start(bf16[27,64,128]{2,1,0:T(8,128)(2,1)} %param.13) | copy-start | bytes 1327108

commit v2 on v1

--- a/solution.py
+++ b/solution.py
@@ -38,14 +38,26 @@
     )
 
 
-def exchange_kernel(
+def column(ea, eb, ec):
+    t = 9 * (ea + 1) + 3 * (eb + 1) + (ec + 1)
+    return t if t < 13 else t - 1
+
+
+def fused_kernel(
     regions,
     blocks,
+    shard,
     counts_ref,
     rebalance_ref,
     owner_ref,
+    neighbors_ref,
     features_ref,
     adjoint_ref,
+    weight_ref,
+    conv_bias_ref,
+    pooled_ref,
+    weight_out,
+    bias_out,
     layers_ref,
     cotangent_ref,
     mine_ref,
@@ -53,15 +65,55 @@
     codes_ref,
     adjoints,
     outgoing,
+    cubes,
+    slabs,
+    stacked,
+    preacts,
+    pooled_block,
+    pooled_in,
+    grad_ref,
+    bias_ref,
+    pooled_got,
+    pooled_sel,
+    pooled_end,
+    pair_got,
+    pair_sum,
+    grad_got,
+    grad_part,
+    grad_slice,
+    grad_full,
+    grad_all,
+    bias_got,
+    bias_part,
     code_sem,
+    lay_send,
+    lay_recv,
     adj_send,
     adj_recv,
+    q_send,
+    q_recv,
+    h_send,
+    h_recv,
+    d_send,
+    d_recv,
+    c_send,
+    c_recv,
     tag_send,
     tag_recv,
-    lay_send,
-    lay_recv,
     cot_send,
     cot_recv,
+    p_send,
+    p_recv,
+    b_send,
+    b_recv,
+    e_send,
+    e_recv,
+    f_send,
+    f_recv,
+    g_send,
+    g_recv,
+    a_send,
+    a_recv,
 ):
     region, block = lax.axis_index("region"), lax.axis_index("block")
     home = features_ref.shape[0]
@@ -91,6 +143,28 @@
     before = lax.rem(block + blocks - 1, blocks)
     after = lax.rem(block + 1, blocks)
     sends = []
+
+    def start(*args):
+        copy = remote(*args)
+        copy.start()
+        sends.append(copy)
+
+    def across(k):
+        return (region, lax.rem(block + k, blocks))
+
+    def along(k):
+        return (lax.rem(region + k, regions), block)
+
+    core, chip, chips = lax.rem(block, 2), lax.div(block, 2), blocks // 2
+    sibling = (region, block + 1 - 2 * core)
+
+    def part(side, j):
+        index = side * chips + lax.rem(chip + j, chips)
+        return pl.ds(pl.multiple_of(index * shard, 16), shard)
+
+    def other_chip(j):
+        return (region, 2 * lax.rem(chip + j, chips) + core)
+
     for k in range(1, regions):
         copy = remote(
             adjoints.at[pl.ds(region * work, work)],
@@ -142,7 +216,7 @@
         ).wait_recv()
     for k in range(1, blocks):
         source = lax.rem(block + blocks - k, blocks)
-        outgoing[source] = adjoints[jnp.maximum(codes_ref[source, 0], 0)]
+        outgoing[source] = adjoints[jnp.clip(codes_ref[source, 0], 0, regions * work - 1)]
         copy = remote(
             outgoing.at[source],
             cotangent_ref.at[block],
@@ -152,50 +226,13 @@
         )
         copy.start()
         sends.append(copy)
-    cotangent_ref[block] = adjoints[jnp.maximum(codes_ref[block, 0], 0)]
+    cotangent_ref[block] = adjoints[jnp.clip(codes_ref[block, 0], 0, regions * work - 1)]
     for i, (slot, target) in enumerate(((2, after), (0, before))):
         remote(
             layers_ref.at[1], layers_ref.at[slot], lay_send.at[i], lay_recv.at[i], (region, target)
         ).wait_recv()
-    for k in range(1, blocks):
-        source = lax.rem(block + blocks - k, blocks)
-        remote(
-            outgoing.at[source],
-            cotangent_ref.at[source],
-            cot_send.at[k],
-            cot_recv.at[k],
-            (region, source),
-        ).wait_recv()
-    for copy in sends:
-        copy.wait_send()
-
-
-def column(ea, eb, ec):
-    t = 9 * (ea + 1) + 3 * (eb + 1) + (ec + 1)
-    return t if t < 13 else t - 1
-
-
-def compute_kernel(
-    blocks,
-    counts_ref,
-    rebalance_ref,
-    neighbors_ref,
-    features_ref,
-    layers_ref,
-    cotangent_ref,
-    weight_ref,
-    bias_ref,
-    pooled_ref,
-    grad_ref,
-    bias_grad_ref,
-    cubes,
-    slabs,
-    stacked,
-    total,
-):
-    home, channels = features_ref.shape[0], features_ref.shape[1]
-    work = home // 2
-    first = (lax.axis_index("region") * blocks + lax.axis_index("block")) * home
+    channels = features_ref.shape[1]
+    first = (region * blocks + block) * home
     voxel = lax.broadcasted_iota(jnp.int32, (1, 512), 1)
     hashed = (voxel * 167) & 511
     for h in range(home):
@@ -204,9 +241,9 @@
             slabs[d * home + h] = layers_ref[d, h].astype(F32)
     cubes[home] = jnp.zeros(cubes.shape[1:], F32)
     slabs[3 * home] = jnp.zeros(slabs.shape[1:], F32)
-    total[...] = jnp.zeros_like(total)
-    bias_grad_ref[...] = jnp.zeros_like(bias_grad_ref)
-    pooled_ref[...] = jnp.zeros_like(pooled_ref)
+    used = weight_ref.shape[0]
+    grad_ref[...] = jnp.zeros_like(grad_ref)
+    bias_ref[...] = jnp.zeros_like(bias_ref)
 
     v = lax.broadcasted_iota(jnp.int32, (512, 64), 0)
     cell = ((v >> 7) * 4 + ((v >> 4) & 3)) * 4 + ((v & 7) >> 1)
@@ -220,17 +257,17 @@
     def shifted(x, offset):
         return pltpu.roll(x, (-offset) % 640, 1)
 
-    def one_block(g, carry):
+    def forward(g, carry):
         def slab(ea, fb, fc):
             target = neighbors_ref[g, column(ea, fb, fc)]
-            return slabs[jnp.where(target >= 0, target - (first - home), 3 * home)]
+            return slabs[jnp.where(target >= 0, jnp.clip(target - (first - home), 0, 3 * home - 1), 3 * home)]
 
         def extended(fb, fc):
             if (fb, fc) == (0, 0):
                 middle = cubes[g]
             else:
                 target = neighbors_ref[g, column(0, fb, fc)]
-                middle = cubes[jnp.where(target >= 0, target - first, home)]
+                middle = cubes[jnp.where(target >= 0, jnp.clip(target - first, 0, home - 1), home)]
             ends = jnp.where(half, slab(1, fb, fc), slab(-1, fb, fc))
             return jnp.concatenate([middle, ends], axis=1)
 
@@ -257,16 +294,16 @@
                 for ea in (-1, 0, 1):
                     tap = 9 * (ea + 1) + 3 * (eb + 1) + (ec + 1)
                     moved = plane if ea == 0 else shifted(plane, 64 * ea)
-                    stacked[tap * channels : (tap + 1) * channels, :] = moved[:, :512].astype(BF16)
+                    stacked[g, tap * channels : (tap + 1) * channels, :] = moved[:, :512].astype(BF16)
 
         preact = (
             lax.dot_general(
                 weight_ref[...],
-                stacked[...],
+                stacked[g],
                 (((0,), (0,)), ((), ())),
                 preferred_element_type=F32,
             )
-            + bias_ref[...]
+            + conv_bias_ref[...]
         )
         live = hashed < counts_ref[g]
         gate = jax.nn.sigmoid(preact)
@@ -276,13 +313,42 @@
         pooled = jnp.dot(high, table, preferred_element_type=F32) + jnp.dot(
             low, table, preferred_element_type=F32
         )
-        line = rebalance_ref[g]
-        device = jnp.where(line >= 0, lax.rem(lax.div(line, work), blocks), blocks)
         middle = pooled.shape[0] // 2
-        pooled_ref[device] = jnp.concatenate([pooled[:middle], pooled[middle:]], axis=1).astype(
+        pooled_block[g] = jnp.concatenate([pooled[:middle], pooled[middle:]], axis=1).astype(
             BF16
         )
-        row = cotangent_ref[jnp.minimum(device, blocks - 1)].astype(F32)
+        preacts[g] = preact
+        return carry
+
+    lax.fori_loop(0, home, forward, 0)
+    for w in range(blocks):
+        slot = 0
+        for h in range(home):
+            line = rebalance_ref[h]
+            hit = (line >= 0) & (lax.rem(lax.div(line, work), blocks) == w)
+            slot = jnp.where(hit, h, slot)
+        pooled_in[w] = pooled_block[slot]
+    for k in range(1, blocks):
+        peer = lax.rem(block + k, blocks)
+        start(pooled_in.at[peer], pooled_got.at[k], p_send.at[k], p_recv.at[k], across(k))
+    pooled_got[0] = pooled_in[block]
+    for k in range(1, blocks):
+        source = lax.rem(block + blocks - k, blocks)
+        remote(
+            outgoing.at[source],
+            cotangent_ref.at[source],
+            cot_send.at[k],
+            cot_recv.at[k],
+            (region, source),
+        ).wait_recv()
+
+    def backward(g, carry):
+        preact = preacts[g]
+        live = hashed < counts_ref[g]
+        gate = jax.nn.sigmoid(preact)
+        line = jnp.maximum(rebalance_ref[g], 0)
+        device = lax.rem(lax.div(line, work), blocks)
+        row = cotangent_ref[device].astype(F32)
         width = row.shape[1] // 2
         row = jnp.concatenate([row[:, :width], row[:, width:]], axis=0).astype(BF16)
         spread = lax.dot_general(
@@ -294,102 +360,23 @@
         grad = jnp.where(live, spread * gate * (1.0 + preact * (1.0 - gate)), 0.0)
         grad_high = grad.astype(BF16)
         grad_low = (grad - grad_high.astype(F32)).astype(BF16)
-        total[...] += lax.dot_general(
-            stacked[...], grad_high, (((1,), (1,)), ((), ())), preferred_element_type=F32
+        grad_ref[:used, :] += lax.dot_general(
+            stacked[g], grad_high, (((1,), (1,)), ((), ())), preferred_element_type=F32
         )
         ones = jnp.ones((8, 512), BF16)
         for part in (grad_high, grad_low):
-            bias_grad_ref[...] += lax.dot_general(
+            bias_ref[...] += lax.dot_general(
                 ones, part, (((1,), (1,)), ((), ())), preferred_element_type=F32
             )
         return carry
 
-    lax.fori_loop(0, home, one_block, 0)
-    used = total.shape[0]
-    grad_ref[:used, :] = total[...]
-    if grad_ref.shape[0] > used:
-        grad_ref[used:, :] = jnp.zeros((grad_ref.shape[0] - used, grad_ref.shape[1]), F32)
-
-
-def reduce_kernel(
-    regions,
-    blocks,
-    shard,
-    pooled_in,
-    codes_ref,
-    grad_ref,
-    bias_ref,
-    pooled_ref,
-    weight_out,
-    bias_out,
-    pooled_got,
-    pooled_sel,
-    pooled_end,
-    pair_got,
-    pair_sum,
-    grad_got,
-    grad_part,
-    grad_slice,
-    grad_full,
-    grad_all,
-    bias_got,
-    bias_part,
-    p_send,
-    p_recv,
-    q_send,
-    q_recv,
-    e_send,
-    e_recv,
-    f_send,
-    f_recv,
-    g_send,
-    g_recv,
-    h_send,
-    h_recv,
-    d_send,
-    d_recv,
-    a_send,
-    a_recv,
-    b_send,
-    b_recv,
-    c_send,
-    c_recv,
-):
-    region, block = lax.axis_index("region"), lax.axis_index("block")
-    work = pooled_ref.shape[0]
-    greet(region, block, regions, blocks)
-    sends = []
-
-    def start(*args):
-        copy = remote(*args)
-        copy.start()
-        sends.append(copy)
-
-    def across(k):
-        return (region, lax.rem(block + k, blocks))
-
-    def along(k):
-        return (lax.rem(region + k, regions), block)
-
-    core, chip, chips = lax.rem(block, 2), lax.div(block, 2), blocks // 2
-    sibling = (region, block + 1 - 2 * core)
-
-    def part(side, j):
-        index = side * chips + lax.rem(chip + j, chips)
-        return pl.ds(pl.multiple_of(index * shard, 16), shard)
-
-    def other_chip(j):
-        return (region, 2 * lax.rem(chip + j, chips) + core)
-
-    for k in range(1, blocks):
-        peer = lax.rem(block + k, blocks)
-        start(pooled_in.at[peer], pooled_got.at[k], p_send.at[k], p_recv.at[k], across(k))
+    lax.fori_loop(0, home, backward, 0)
+    for k in range(1, blocks):
         start(bias_ref, bias_got.at[k], b_send.at[k], b_recv.at[k], across(k))
     for j in (*range(1, chips), 0):
         start(
             grad_ref.at[part(1 - core, j)], pair_got.at[j], e_send.at[j], e_recv.at[j], sibling
         )
-    pooled_got[0] = pooled_in[block]
     for j in (*range(1, chips), 0):
         remote(
             grad_ref.at[part(1 - core, j)], pair_got.at[j], e_send.at[j], e_recv.at[j], sibling
@@ -520,74 +507,31 @@
     dma = pltpu.SemaphoreType.DMA
     shape = jax.ShapeDtypeStruct
 
-    layers, cotangent, codes = pl.pallas_call(
-        functools.partial(exchange_kernel, regions, blocks),
-        out_shape=(
-            shape((3, home, channels, 128), BF16),
-            shape((blocks,) + dense, BF16),
-            shape((blocks, 128), jnp.int32),
-        ),
-        in_specs=[smem, smem, smem, vmem, vmem],
-        out_specs=(vmem, vmem, vmem),
-        scratch_shapes=[
-            pltpu.VMEM((blocks, blocks, 128), jnp.int32),
-            pltpu.SMEM((blocks, 128), jnp.int32),
-            pltpu.VMEM((regions * work,) + dense, BF16),
-            pltpu.VMEM((blocks,) + dense, BF16),
-            dma,
-            dma((regions,)),
-            dma((regions,)),
-            dma((blocks,)),
-            dma((blocks,)),
-            dma((2,)),
-            dma((2,)),
-            dma((blocks,)),
-            dma((blocks,)),
-        ],
-        compiler_params=pltpu.CompilerParams(
-            collective_id=0, has_side_effects=True, vmem_limit_bytes=VMEM_LIMIT
-        ),
-        name="exchange",
-    )(counts, rebalance, coarse_owner, features, merged_adjoint.reshape(work, outs, cells))
-
-    pooled_send, grad_send, bias_send = pl.pallas_call(
-        functools.partial(compute_kernel, blocks),
-        out_shape=(
-            shape((blocks + 1,) + dense, BF16),
-            shape((blocks * shard, outs), F32),
-            shape((8, outs), F32),
-        ),
-        in_specs=[smem, smem, smem, vmem, vmem, vmem, vmem, vmem],
-        out_specs=(vmem, vmem, vmem),
-        scratch_shapes=[
-            pltpu.VMEM((home + 1, channels, 512), F32),
-            pltpu.VMEM((3 * home + 1, channels, 128), F32),
-            pltpu.VMEM((rows, 512), BF16),
-            pltpu.VMEM((rows, outs), F32),
-        ],
-        compiler_params=pltpu.CompilerParams(vmem_limit_bytes=VMEM_LIMIT),
-        name="convolve",
-    )(
-        counts,
-        rebalance,
-        neighbors,
-        features,
-        layers,
-        cotangent,
-        conv_weight.reshape(rows, outs),
-        convolution_bias_vector.reshape(outs, 1),
-    )
-
     pooled, weight_total, bias_total = pl.pallas_call(
-        functools.partial(reduce_kernel, regions, blocks, shard),
+        functools.partial(fused_kernel, regions, blocks, shard),
         out_shape=(
             shape((work, outs, cells), BF16),
             shape((rows, outs), F32),
             shape((8, outs), F32),
         ),
-        in_specs=[vmem, smem, vmem, vmem],
+        in_specs=[smem] * 4 + [vmem] * 4,
         out_specs=(vmem, vmem, vmem),
         scratch_shapes=[
+            pltpu.VMEM((3, home, channels, 128), BF16),
+            pltpu.VMEM((blocks,) + dense, BF16),
+            pltpu.VMEM((blocks, 128), jnp.int32),
+            pltpu.VMEM((blocks, blocks, 128), jnp.int32),
+            pltpu.SMEM((blocks, 128), jnp.int32),
+            pltpu.VMEM((regions * work,) + dense, BF16),
+            pltpu.VMEM((blocks,) + dense, BF16),
+            pltpu.VMEM((home + 1, channels, 512), F32),
+            pltpu.VMEM((3 * home + 1, channels, 128), F32),
+            pltpu.VMEM((home, rows, 512), BF16),
+            pltpu.VMEM((home, outs, 512), F32),
+            pltpu.VMEM((home,) + dense, BF16),
+            pltpu.VMEM((blocks,) + dense, BF16),
+            pltpu.VMEM((blocks * shard, outs), F32),
+            pltpu.VMEM((8, outs), F32),
             pltpu.VMEM((blocks,) + dense, BF16),
             pltpu.VMEM((regions, work) + dense, BF16),
             pltpu.VMEM((regions, work) + dense, BF16),
@@ -600,32 +544,27 @@
             pltpu.VMEM((2, chips, shard, outs), BF16),
             pltpu.VMEM((blocks, 8, outs), F32),
             pltpu.VMEM((regions, 8, outs), F32),
-            dma((blocks,)),
-            dma((blocks,)),
-            dma((regions,)),
-            dma((regions,)),
-            dma((chips,)),
-            dma((chips,)),
-            dma((chips,)),
-            dma((chips,)),
-            dma((chips,)),
-            dma((chips,)),
-            dma((regions,)),
-            dma((regions,)),
-            dma((regions,)),
-            dma((regions,)),
-            dma((chips,)),
-            dma((chips,)),
-            dma((blocks,)),
-            dma((blocks,)),
-            dma((regions,)),
-            dma((regions,)),
-        ],
+            dma,
+            dma((2,)),
+            dma((2,)),
+        ]
+        + [dma((regions,))] * 10
+        + [dma((blocks,))] * 8
+        + [dma((chips,))] * 8,
         compiler_params=pltpu.CompilerParams(
-            collective_id=1, has_side_effects=True, vmem_limit_bytes=VMEM_LIMIT
+            collective_id=0, has_side_effects=True, vmem_limit_bytes=VMEM_LIMIT
         ),
-        name="reduce",
-    )(pooled_send, codes, grad_send, bias_send)
+        name="fused",
+    )(
+        counts,
+        rebalance,
+        coarse_owner,
+        neighbors,
+        features,
+        merged_adjoint.reshape(work, outs, cells),
+        conv_weight.reshape(rows, outs),
+        convolution_bias_vector.reshape(outs, 1),
+    )
     return (
         pooled.reshape(work, outs * cells),
         weight_total.reshape(taps, channels, outs),

time: 56.4 us -> 49.4 us (0.88)
  Pallas kernels: 48.6 us -> 42.2 us
  local copies, waits for them, and re-layouts: 6.87 us -> 6.21 us
    pallas_call x3 -> x1, Pallas kernels: 48.6 us -> 42.2 us  [per_device(): pl.pallas_call(functools.partial(fused_kernel, regions, blocks, shard), o...]
    unnamed x19 -> x17, local copies, waits for them, and re-layouts: 5.41 us -> 4.75 us
where the time goes in v2:
time: 49.4 us; the launch traced here: 49.1 us
  Pallas kernels  42.2 us (85%)
  local copies, waits for them, and re-layouts  6.21 us (13%)
  between operations  0.66 us (1%)
    pallas_call x1, Pallas kernels, per_device(): pl.pallas_call(functools.partial(fused_kernel, regions, blocks, shard), o...  42.2 us
    unnamed x17, local copies, waits for them, and re-layouts  4.75 us

profile of v2, /device:TPU:1, one launch (start us, length us, event | category | flops | bytes accessed | tf_op | source)
XLA Modules:
  0.0 49.1 jit_solution(364485878646400596)
XLA Ops:
  0.6 0.0 copy-start.7
  0.6 0.6 %copy-done.7 = f32[128]{0:T(128)S(1)} copy-done((f32[128]{0:T(128)S(1)}, f32[128]{0:T(128)}, u32[]{:S(2)}) %copy-start.7) | copy-done | bytes 536
  1.3 0.0 copy-start.6
  1.3 0.1 copy.12.conv_bias_ref
  1.4 0.6 %copy-done.6 = bf16[2,8192]{1,0:T(2,128)(2,1)S(1)} copy-done((bf16[2,8192]{1,0:T(2,128)(2,1)S(1)}, bf16[2,8192]{1,0:T(2,128)(2,1)}, u32[]{:S(2)}) %copy-start.6) | copy-done | bytes 32792
  2.0 0.0 copy-start.2
  2.0 0.0 copy-start.3
  2.0 0.0 copy-start.4
  2.1 0.0 copy-start.5
  2.1 0.1 reshape.21.adjoint_ref
  2.2 0.6 %copy-done.2 = s32[4,26]{1,0:T(4,128)S(1)} copy-done((s32[4,26]{1,0:T(4,128)S(1)}, s32[4,26]{1,0:T(4,128)}, u32[]{:S(2)}) %copy-start.2) | copy-done | bytes 440
  2.7 0.0 copy-done.3
  2.7 0.0 copy-done.4
  2.7 0.0 copy-done.5
  2.7 0.0 copy-start
  2.8 1.0 %copy-done = bf16[27,64,128]{2,1,0:T(8,128)(2,1)S(1)} copy-done((bf16[27,64,128]{2,1,0:T(8,128)(2,1)S(1)}, bf16[27,64,128]{2,1,0:T(8,128)(2,1)}, u32[]{:S(2)}) %copy-start) | copy-done | bytes 442392
  3.8 0.0 copy-start.1
  3.8 0.9 %copy-done.1 = bf16[4,64,512]{2,1,0:T(8,128)(2,1)S(1)} copy-done((bf16[4,64,512]{2,1,0:T(8,128)(2,1)S(1)}, bf16[4,64,512]{2,1,0:T(8,128)(2,1)}, u32[]{:S(2)}) %copy-start.1) | copy-done | bytes 262168
  4.7 42.2 %fused.1 = (bf16[2,128,64]{2,1,0:T(8,128)(2,1)S(1)}, f32[1728,128]{1,0:T(8,128)S(1)}, f32[8,128]{1,0:T(8,128)S(1)}) custom-call(s32[4]{0:T(128)S(1)} %copy-done.3, s32[4]{0:T(128)S(1)} %copy-done.4, s32[4]{0:T(128)S(1)} %copy-done.5, s32[4,26]{1,0:T(4,128)S(1)} %copy-done.2, bf16[4,64,512]{2,1,0:T(8,128)(2,1)S(1)} %copy-done.1, ...), custom_call_target="tpu_custom_call" | custom-call | tf_op jit(solution)/shard_map/fused/pallas_call | solution.py:510
  46.9 0.7 %reshape.24 = bf16[2,8192]{1,0:T(2,128)(2,1)} reshape(bf16[2,128,64]{2,1,0:T(8,128)(2,1)S(1)} %get-tuple-element.6) | data formatting | bytes 65536 | tf_op jit(solution)/shard_map/reshape | solution.py:569
  47.6 0.5 %slice_bitcast_fusion = f32[128]{0:T(128)} fusion(f32[8,128]{1,0:T(8,128)S(1)} %get-tuple-element.8), kind=kLoop, calls=%fused_computation | loop fusion | bytes 1024 | tf_op jit(solution)/shard_map/squeeze | solution.py:571
  48.1 0.9 %copy.14 = f32[27,64,128]{2,1,0:T(8,128)} copy(f32[27,64,128]{2,1,0:T(8,128)S(1)} %bitcast.5) | data formatting | bytes 1769472
Async XLA Ops:
  0.6 0.7 %copy-start.7 = (f32[128]{0:T(128)S(1)}, f32[128]{0:T(128)}, u32[]{:S(2)}) copy-start(f32[128]{0:T(128)} %param.14) | copy-start | bytes 1540
  1.3 0.8 %copy-start.6 = (bf16[2,8192]{1,0:T(2,128)(2,1)S(1)}, bf16[2,8192]{1,0:T(2,128)(2,1)}, u32[]{:S(2)}) copy-start(bf16[2,8192]{1,0:T(2,128)(2,1)} %param.15) | copy-start | bytes 98308
  2.0 0.7 %copy-start.2 = (s32[4,26]{1,0:T(4,128)S(1)}, s32[4,26]{1,0:T(4,128)}, u32[]{:S(2)}) copy-start(s32[4,26]{1,0:T(4,128)} %neighbors_ref.1) | copy-start | bytes 1252
  2.0 0.7 %copy-start.3 = (s32[4]{0:T(128)S(1)}, s32[4]{0:T(128)}, u32[]{:S(2)}) copy-start(s32[4]{0:T(128)} %counts_ref.1) | copy-start | bytes 52
  2.0 0.7 %copy-start.4 = (s32[4]{0:T(128)S(1)}, s32[4]{0:T(128)}, u32[]{:S(2)}) copy-start(s32[4]{0:T(128)} %rebalance_ref.1) | copy-start | bytes 52
  2.1 0.7 %copy-start.5 = (s32[4]{0:T(128)S(1)}, s32[4]{0:T(128)}, u32[]{:S(2)}) copy-start(s32[4]{0:T(128)} %owner_ref.1) | copy-start | bytes 52
  2.7 1.0 %copy-start = (bf16[27,64,128]{2,1,0:T(8,128)(2,1)S(1)}, bf16[27,64,128]{2,1,0:T(8,128)(2,1)}, u32[]{:S(2)}) copy-start(bf16[27,64,128]{2,1,0:T(8,128)(2,1)} %param.13) | copy-start | bytes 1327108
  3.8 0.9 %copy-start.1 = (bf16[4,64,512]{2,1,0:T(8,128)(2,1)S(1)}, bf16[4,64,512]{2,1,0:T(8,128)(2,1)}, u32[]{:S(2)}) copy-start(bf16[4,64,512]{2,1,0:T(8,128)(2,1)} %features_ref.1) | copy-start | bytes 786436

commit v3 on v2

--- a/solution.py
+++ b/solution.py
@@ -53,11 +53,13 @@
     neighbors_ref,
     features_ref,
     adjoint_ref,
-    weight_ref,
+    weight_hbm,
     conv_bias_ref,
     pooled_ref,
     weight_out,
     bias_out,
+    weight_ref,
+    grads,
     layers_ref,
     cotangent_ref,
     mine_ref,
@@ -85,6 +87,7 @@
     grad_all,
     bias_got,
     bias_part,
+    weight_sem,
     code_sem,
     lay_send,
     lay_recv,
@@ -115,6 +118,8 @@
     a_send,
     a_recv,
 ):
+    weight_copy = pltpu.make_async_copy(weight_hbm, weight_ref, weight_sem)
+    weight_copy.start()
     region, block = lax.axis_index("region"), lax.axis_index("block")
     home = features_ref.shape[0]
     work = adjoint_ref.shape[0]
@@ -191,42 +196,6 @@
         )
         copy.start()
         sends.append(copy)
-    for k in range(1, blocks):
-        source = lax.rem(block + blocks - k, blocks)
-        remote(
-            tags_ref.at[source],
-            tags_ref.at[source],
-            tag_send.at[k],
-            tag_recv.at[k],
-            (region, source),
-        ).wait_recv()
-        mine_ref[pl.ds(source, 1), :] = tags_ref[source, pl.ds(block, 1), :]
-    mine_ref[pl.ds(block, 1), :] = tags_ref[block, pl.ds(block, 1), :]
-    codes_copy = pltpu.make_async_copy(mine_ref, codes_ref, code_sem)
-    codes_copy.start()
-    codes_copy.wait()
-    for k in range(1, regions):
-        source = lax.rem(region + regions - k, regions)
-        remote(
-            adjoints.at[pl.ds(source * work, work)],
-            adjoints.at[pl.ds(source * work, work)],
-            adj_send.at[k],
-            adj_recv.at[k],
-            (source, block),
-        ).wait_recv()
-    for k in range(1, blocks):
-        source = lax.rem(block + blocks - k, blocks)
-        outgoing[source] = adjoints[jnp.clip(codes_ref[source, 0], 0, regions * work - 1)]
-        copy = remote(
-            outgoing.at[source],
-            cotangent_ref.at[block],
-            cot_send.at[blocks - k],
-            cot_recv.at[blocks - k],
-            (region, source),
-        )
-        copy.start()
-        sends.append(copy)
-    cotangent_ref[block] = adjoints[jnp.clip(codes_ref[block, 0], 0, regions * work - 1)]
     for i, (slot, target) in enumerate(((2, after), (0, before))):
         remote(
             layers_ref.at[1], layers_ref.at[slot], lay_send.at[i], lay_recv.at[i], (region, target)
@@ -242,7 +211,9 @@
     cubes[home] = jnp.zeros(cubes.shape[1:], F32)
     slabs[3 * home] = jnp.zeros(slabs.shape[1:], F32)
     used = weight_ref.shape[0]
-    grad_ref[...] = jnp.zeros_like(grad_ref)
+    if stacked.shape[1] > used:
+        for h in range(home):
+            stacked[h, used:, :] = jnp.zeros((stacked.shape[1] - used, 512), BF16)
     bias_ref[...] = jnp.zeros_like(bias_ref)
 
     v = lax.broadcasted_iota(jnp.int32, (512, 64), 0)
@@ -299,7 +270,7 @@
         preact = (
             lax.dot_general(
                 weight_ref[...],
-                stacked[g],
+                stacked[g, :used, :],
                 (((0,), (0,)), ((), ())),
                 preferred_element_type=F32,
             )
@@ -320,7 +291,45 @@
         preacts[g] = preact
         return carry
 
-    lax.fori_loop(0, home, forward, 0)
+    weight_copy.wait()
+    lax.fori_loop(0, 1, forward, 0)
+    for k in range(1, blocks):
+        source = lax.rem(block + blocks - k, blocks)
+        remote(
+            tags_ref.at[source],
+            tags_ref.at[source],
+            tag_send.at[k],
+            tag_recv.at[k],
+            (region, source),
+        ).wait_recv()
+        mine_ref[pl.ds(source, 1), :] = tags_ref[source, pl.ds(block, 1), :]
+    mine_ref[pl.ds(block, 1), :] = tags_ref[block, pl.ds(block, 1), :]
+    codes_copy = pltpu.make_async_copy(mine_ref, codes_ref, code_sem)
+    codes_copy.start()
+    codes_copy.wait()
+    for k in range(1, regions):
+        source = lax.rem(region + regions - k, regions)
+        remote(
+            adjoints.at[pl.ds(source * work, work)],
+            adjoints.at[pl.ds(source * work, work)],
+            adj_send.at[k],
+            adj_recv.at[k],
+            (source, block),
+        ).wait_recv()
+    for k in range(1, blocks):
+        source = lax.rem(block + blocks - k, blocks)
+        outgoing[source] = adjoints[jnp.clip(codes_ref[source, 0], 0, regions * work - 1)]
+        copy = remote(
+            outgoing.at[source],
+            cotangent_ref.at[block],
+            cot_send.at[blocks - k],
+            cot_recv.at[blocks - k],
+            (region, source),
+        )
+        copy.start()
+        sends.append(copy)
+    cotangent_ref[block] = adjoints[jnp.clip(codes_ref[block, 0], 0, regions * work - 1)]
+    lax.fori_loop(1, home, forward, 0)
     for w in range(blocks):
         slot = 0
         for h in range(home):
@@ -360,9 +369,7 @@
         grad = jnp.where(live, spread * gate * (1.0 + preact * (1.0 - gate)), 0.0)
         grad_high = grad.astype(BF16)
         grad_low = (grad - grad_high.astype(F32)).astype(BF16)
-        grad_ref[:used, :] += lax.dot_general(
-            stacked[g], grad_high, (((1,), (1,)), ((), ())), preferred_element_type=F32
-        )
+        grads[g] = grad_high
         ones = jnp.ones((8, 512), BF16)
         for part in (grad_high, grad_low):
             bias_ref[...] += lax.dot_general(
@@ -373,15 +380,30 @@
     lax.fori_loop(0, home, backward, 0)
     for k in range(1, blocks):
         start(bias_ref, bias_got.at[k], b_send.at[k], b_recv.at[k], across(k))
+
+    def slice_of(side, j):
+        rows = part(side, j)
+        total = jnp.zeros((shard, grad_ref.shape[1]), F32)
+        for h in range(home):
+            total = total + lax.dot_general(
+                stacked[h, rows, :],
+                grads[h],
+                (((1,), (1,)), ((), ())),
+                preferred_element_type=F32,
+            )
+        return total
+
     for j in (*range(1, chips), 0):
+        grad_ref[part(1 - core, j), :] = slice_of(1 - core, j)
         start(
             grad_ref.at[part(1 - core, j)], pair_got.at[j], e_send.at[j], e_recv.at[j], sibling
         )
     for j in (*range(1, chips), 0):
+        grad_sum = slice_of(core, j)
         remote(
             grad_ref.at[part(1 - core, j)], pair_got.at[j], e_send.at[j], e_recv.at[j], sibling
         ).wait_recv()
-        grad_sum = grad_ref[part(core, j), :] + pair_got[j]
+        grad_sum = grad_sum + pair_got[j]
         if j > 0:
             pair_sum[j] = grad_sum.astype(BF16)
             start(pair_sum.at[j], grad_got.at[j], g_send.at[j], g_recv.at[j], other_chip(j))
@@ -514,9 +536,11 @@
             shape((rows, outs), F32),
             shape((8, outs), F32),
         ),
-        in_specs=[smem] * 4 + [vmem] * 4,
+        in_specs=[smem] * 4 + [vmem, vmem, pl.BlockSpec(memory_space=pl.ANY), vmem],
         out_specs=(vmem, vmem, vmem),
         scratch_shapes=[
+            pltpu.VMEM((rows, outs), BF16),
+            pltpu.VMEM((home, outs, 512), BF16),
             pltpu.VMEM((3, home, channels, 128), BF16),
             pltpu.VMEM((blocks,) + dense, BF16),
             pltpu.VMEM((blocks, 128), jnp.int32),
@@ -526,7 +550,7 @@
             pltpu.VMEM((blocks,) + dense, BF16),
             pltpu.VMEM((home + 1, channels, 512), F32),
             pltpu.VMEM((3 * home + 1, channels, 128), F32),
-            pltpu.VMEM((home, rows, 512), BF16),
+            pltpu.VMEM((home, blocks * shard, 512), BF16),
             pltpu.VMEM((home, outs, 512), F32),
             pltpu.VMEM((home,) + dense, BF16),
             pltpu.VMEM((blocks,) + dense, BF16),
@@ -544,6 +568,7 @@
             pltpu.VMEM((2, chips, shard, outs), BF16),
             pltpu.VMEM((blocks, 8, outs), F32),
             pltpu.VMEM((regions, 8, outs), F32),
+            dma,
             dma,
             dma((2,)),
             dma((2,)),

time: 49.4 us -> 49.6 us (level)
  no operation moved by 1% of the time
where the time goes in v3:
time: 49.6 us; the launch traced here: 49.3 us
  Pallas kernels  42.5 us (86%)
  local copies, waits for them, and re-layouts  6.21 us (13%)
  between operations  0.66 us (1%)
    pallas_call x1, Pallas kernels, per_device(): pl.pallas_call(functools.partial(fused_kernel, regions, blocks, shard), o...  42.5 us
    unnamed x17, local copies, waits for them, and re-layouts  4.75 us

profile of v3, /device:TPU:1, one launch (start us, length us, event | category | flops | bytes accessed | tf_op | source)
XLA Modules:
  0.0 49.3 jit_solution(2320230635684889804)
XLA Ops:
  0.6 0.0 copy-start.7
  0.6 0.6 %copy-done.7 = f32[128]{0:T(128)S(1)} copy-done((f32[128]{0:T(128)S(1)}, f32[128]{0:T(128)}, u32[]{:S(2)}) %copy-start.7) | copy-done | bytes 536
  1.3 0.0 copy-start.6
  1.3 0.1 copy.12.conv_bias_ref
  1.4 0.6 %copy-done.6 = bf16[2,8192]{1,0:T(2,128)(2,1)S(1)} copy-done((bf16[2,8192]{1,0:T(2,128)(2,1)S(1)}, bf16[2,8192]{1,0:T(2,128)(2,1)}, u32[]{:S(2)}) %copy-start.6) | copy-done | bytes 32792
  2.0 0.0 copy-start.2
  2.0 0.0 copy-start.3
  2.0 0.0 copy-start.4
  2.1 0.0 copy-start.5
  2.1 0.1 reshape.21.adjoint_ref
  2.2 0.6 %copy-done.2 = s32[4,26]{1,0:T(4,128)S(1)} copy-done((s32[4,26]{1,0:T(4,128)S(1)}, s32[4,26]{1,0:T(4,128)}, u32[]{:S(2)}) %copy-start.2) | copy-done | bytes 440
  2.7 0.0 copy-done.3
  2.7 0.0 copy-done.4
  2.7 0.0 copy-done.5
  2.7 0.0 copy-start
  2.8 1.0 %copy-done = bf16[27,64,128]{2,1,0:T(8,128)(2,1)S(1)} copy-done((bf16[27,64,128]{2,1,0:T(8,128)(2,1)S(1)}, bf16[27,64,128]{2,1,0:T(8,128)(2,1)}, u32[]{:S(2)}) %copy-start) | copy-done | bytes 442392
  3.8 0.0 copy-start.1
  3.8 0.9 %copy-done.1 = bf16[4,64,512]{2,1,0:T(8,128)(2,1)S(1)} copy-done((bf16[4,64,512]{2,1,0:T(8,128)(2,1)S(1)}, bf16[4,64,512]{2,1,0:T(8,128)(2,1)}, u32[]{:S(2)}) %copy-start.1) | copy-done | bytes 262168
  4.7 42.5 %fused.1 = (bf16[2,128,64]{2,1,0:T(8,128)(2,1)S(1)}, f32[1728,128]{1,0:T(8,128)S(1)}, f32[8,128]{1,0:T(8,128)S(1)}) custom-call(s32[4]{0:T(128)S(1)} %copy-done.3, s32[4]{0:T(128)S(1)} %copy-done.4, s32[4]{0:T(128)S(1)} %copy-done.5, s32[4,26]{1,0:T(4,128)S(1)} %copy-done.2, bf16[4,64,512]{2,1,0:T(8,128)(2,1)S(1)} %copy-done.1, ...), custom_call_target="tpu_custom_call" | custom-call | tf_op jit(solution)/shard_map/fused/pallas_call | solution.py:532
  47.2 0.7 %reshape.24 = bf16[2,8192]{1,0:T(2,128)(2,1)} reshape(bf16[2,128,64]{2,1,0:T(8,128)(2,1)S(1)} %get-tuple-element.6) | data formatting | bytes 65536 | tf_op jit(solution)/shard_map/reshape | solution.py:594
  47.9 0.5 %slice_bitcast_fusion = f32[128]{0:T(128)} fusion(f32[8,128]{1,0:T(8,128)S(1)} %get-tuple-element.8), kind=kLoop, calls=%fused_computation | loop fusion | bytes 1024 | tf_op jit(solution)/shard_map/squeeze | solution.py:596
  48.4 0.9 %copy.14 = f32[27,64,128]{2,1,0:T(8,128)} copy(f32[27,64,128]{2,1,0:T(8,128)S(1)} %bitcast.5) | data formatting | bytes 1769472
Async XLA Ops:
  0.6 0.7 %copy-start.7 = (f32[128]{0:T(128)S(1)}, f32[128]{0:T(128)}, u32[]{:S(2)}) copy-start(f32[128]{0:T(128)} %param.14) | copy-start | bytes 1540
  1.3 0.8 %copy-start.6 = (bf16[2,8192]{1,0:T(2,128)(2,1)S(1)}, bf16[2,8192]{1,0:T(2,128)(2,1)}, u32[]{:S(2)}) copy-start(bf16[2,8192]{1,0:T(2,128)(2,1)} %param.15) | copy-start | bytes 98308
  2.0 0.7 %copy-start.2 = (s32[4,26]{1,0:T(4,128)S(1)}, s32[4,26]{1,0:T(4,128)}, u32[]{:S(2)}) copy-start(s32[4,26]{1,0:T(4,128)} %neighbors_ref.1) | copy-start | bytes 1252
  2.0 0.7 %copy-start.3 = (s32[4]{0:T(128)S(1)}, s32[4]{0:T(128)}, u32[]{:S(2)}) copy-start(s32[4]{0:T(128)} %counts_ref.1) | copy-start | bytes 52
  2.0 0.7 %copy-start.4 = (s32[4]{0:T(128)S(1)}, s32[4]{0:T(128)}, u32[]{:S(2)}) copy-start(s32[4]{0:T(128)} %rebalance_ref.1) | copy-start | bytes 52
  2.1 0.7 %copy-start.5 = (s32[4]{0:T(128)S(1)}, s32[4]{0:T(128)}, u32[]{:S(2)}) copy-start(s32[4]{0:T(128)} %owner_ref.1) | copy-start | bytes 52
  2.7 1.0 %copy-start = (bf16[27,64,128]{2,1,0:T(8,128)(2,1)S(1)}, bf16[27,64,128]{2,1,0:T(8,128)(2,1)}, u32[]{:S(2)}) copy-start(bf16[27,64,128]{2,1,0:T(8,128)(2,1)} %param.13) | copy-start | bytes 1327108
  3.8 0.9 %copy-start.1 = (bf16[4,64,512]{2,1,0:T(8,128)(2,1)S(1)}, bf16[4,64,512]{2,1,0:T(8,128)(2,1)}, u32[]{:S(2)}) copy-start(bf16[4,64,512]{2,1,0:T(8,128)(2,1)} %features_ref.1) | copy-start | bytes 786436

commit v4 on v2

--- a/solution.py
+++ b/solution.py
@@ -257,6 +257,14 @@
     def shifted(x, offset):
         return pltpu.roll(x, (-offset) % 640, 1)
 
+    outs = conv_bias_ref.shape[1]
+    diagonal = lax.broadcasted_iota(jnp.int32, (outs, outs), 0) == lax.broadcasted_iota(
+        jnp.int32, (outs, outs), 1
+    )
+    bias_column = jnp.sum(
+        jnp.where(diagonal, conv_bias_ref[...], 0.0), axis=1, keepdims=True
+    )
+
     def forward(g, carry):
         def slab(ea, fb, fc):
             target = neighbors_ref[g, column(ea, fb, fc)]
@@ -303,7 +311,7 @@
                 (((0,), (0,)), ((), ())),
                 preferred_element_type=F32,
             )
-            + conv_bias_ref[...]
+            + bias_column
         )
         live = hashed < counts_ref[g]
         gate = jax.nn.sigmoid(preact)
@@ -462,7 +470,7 @@
     bias_sum = bias_part[0]
     for r in range(1, regions):
         bias_sum = bias_sum + bias_part[r]
-    bias_out[...] = bias_sum
+    bias_out[...] = bias_sum[:1]
     for s in range(work):
         rows = pooled_sel[region, s].astype(F32)
         for k in range(1, regions):
@@ -512,7 +520,7 @@
         out_shape=(
             shape((work, outs, cells), BF16),
             shape((rows, outs), F32),
-            shape((8, outs), F32),
+            shape((1, outs), F32),
         ),
         in_specs=[smem] * 4 + [vmem] * 4,
         out_specs=(vmem, vmem, vmem),
@@ -563,12 +571,12 @@
         features,
         merged_adjoint.reshape(work, outs, cells),
         conv_weight.reshape(rows, outs),
-        convolution_bias_vector.reshape(outs, 1),
+        convolution_bias_vector.reshape(1, outs),
     )
     return (
         pooled.reshape(work, outs * cells),
         weight_total.reshape(taps, channels, outs),
-        bias_total[0],
+        bias_total.reshape(outs),
     )
 
 

time: 49.4 us -> 48.2 us (0.976)
  local copies, waits for them, and re-layouts: 6.21 us -> 5.03 us
    unnamed x17 -> x16, local copies, waits for them, and re-layouts: 4.75 us -> 3.4 us
    reshape x1, local copies, waits for them, and re-layouts: 0.11 us -> 0.9 us  [per_device(): merged_adjoint.reshape(work, outs, cells)]
    squeeze x1 -> x0, local copies, waits for them, and re-layouts: 0.51 us -> none  [per_device(): bias_total[0]]
where the time goes in v4:
time: 48.2 us; the launch traced here: 48 us
  Pallas kernels  42.2 us (88%)
  local copies, waits for them, and re-layouts  5.03 us (10%)
  between operations  0.73 us (2%)
    pallas_call x1, Pallas kernels, per_device(): pl.pallas_call(functools.partial(fused_kernel, regions, blocks, shard), o...  42.2 us
    unnamed x16, local copies, waits for them, and re-layouts  3.4 us

profile of v4, /device:TPU:1, one launch (start us, length us, event | category | flops | bytes accessed | tf_op | source)
XLA Modules:
  0.0 48.0 jit_solution(16258452481607555669)
XLA Ops:
  0.6 0.0 copy-start.2
  0.6 0.0 copy-start.3
  0.7 0.0 copy-start.4
  0.7 0.0 copy-start.5
  0.7 0.0 copy-start.6
  0.7 0.9 %reshape.24.adjoint_ref = bf16[2,128,64]{2,1,0:T(8,128)(2,1)S(1)} reshape(bf16[2,8192]{1,0:T(2,128)(2,1)} %param.15) | data formatting | bytes 65536 | tf_op jit(solution)/shard_map/reshape | solution.py:572
  1.6 0.0 copy-done.2
  1.6 0.0 copy-done.3
  1.6 0.0 copy-done.4
  1.6 0.0 copy-done.5
  1.6 0.0 copy-done.6
  1.6 0.0 copy-start
  1.6 1.0 %copy-done = bf16[27,64,128]{2,1,0:T(8,128)(2,1)S(1)} copy-done((bf16[27,64,128]{2,1,0:T(8,128)(2,1)S(1)}, bf16[27,64,128]{2,1,0:T(8,128)(2,1)}, u32[]{:S(2)}) %copy-start) | copy-done | bytes 442392
  2.6 0.0 copy-start.1
  2.6 0.9 %copy-done.1 = bf16[4,64,512]{2,1,0:T(8,128)(2,1)S(1)} copy-done((bf16[4,64,512]{2,1,0:T(8,128)(2,1)S(1)}, bf16[4,64,512]{2,1,0:T(8,128)(2,1)}, u32[]{:S(2)}) %copy-start.1) | copy-done | bytes 262168
  3.6 42.2 %fused.1 = (bf16[2,128,64]{2,1,0:T(8,128)(2,1)S(1)}, f32[1728,128]{1,0:T(8,128)S(1)}, f32[1,128]{1,0:T(1,128)S(1)}) custom-call(s32[4]{0:T(128)S(1)} %copy-done.3, s32[4]{0:T(128)S(1)} %copy-done.4, s32[4]{0:T(128)S(1)} %copy-done.5, s32[4,26]{1,0:T(4,128)S(1)} %copy-done.2, bf16[4,64,512]{2,1,0:T(8,128)(2,1)S(1)} %copy-done.1, ...), custom_call_target="tpu_custom_call" | custom-call | tf_op jit(solution)/shard_map/fused/pallas_call | solution.py:518
  45.8 0.7 %reshape.27 = bf16[2,8192]{1,0:T(2,128)(2,1)} reshape(bf16[2,128,64]{2,1,0:T(8,128)(2,1)S(1)} %get-tuple-element.6) | data formatting | bytes 65536 | tf_op jit(solution)/shard_map/reshape | solution.py:577
  46.5 0.9 %copy.13 = f32[27,64,128]{2,1,0:T(8,128)} copy(f32[27,64,128]{2,1,0:T(8,128)S(1)} %bitcast.4) | data formatting | bytes 1769472
  47.4 0.5 %copy.14 = f32[128]{0:T(128)} copy(f32[128]{0:T(128)S(1)} %bitcast.7) | data formatting | bytes 1024
Async XLA Ops:
  0.6 1.0 %copy-start.2 = (s32[4,26]{1,0:T(4,128)S(1)}, s32[4,26]{1,0:T(4,128)}, u32[]{:S(2)}) copy-start(s32[4,26]{1,0:T(4,128)} %neighbors_ref.1) | copy-start | bytes 1252
  0.6 1.0 %copy-start.3 = (s32[4]{0:T(128)S(1)}, s32[4]{0:T(128)}, u32[]{:S(2)}) copy-start(s32[4]{0:T(128)} %counts_ref.1) | copy-start | bytes 52
  0.7 1.0 %copy-start.4 = (s32[4]{0:T(128)S(1)}, s32[4]{0:T(128)}, u32[]{:S(2)}) copy-start(s32[4]{0:T(128)} %rebalance_ref.1) | copy-start | bytes 52
  0.7 1.0 %copy-start.5 = (s32[4]{0:T(128)S(1)}, s32[4]{0:T(128)}, u32[]{:S(2)}) copy-start(s32[4]{0:T(128)} %owner_ref.1) | copy-start | bytes 52
  0.7 1.0 %copy-start.6 = (f32[128]{0:T(128)S(1)}, f32[128]{0:T(128)}, u32[]{:S(2)}) copy-start(f32[128]{0:T(128)} %param.14) | copy-start | bytes 1540
  1.6 1.0 %copy-start = (bf16[27,64,128]{2,1,0:T(8,128)(2,1)S(1)}, bf16[27,64,128]{2,1,0:T(8,128)(2,1)}, u32[]{:S(2)}) copy-start(bf16[27,64,128]{2,1,0:T(8,128)(2,1)} %param.13) | copy-start | bytes 1327108
  2.6 0.9 %copy-start.1 = (bf16[4,64,512]{2,1,0:T(8,128)(2,1)S(1)}, bf16[4,64,512]{2,1,0:T(8,128)(2,1)}, u32[]{:S(2)}) copy-start(bf16[4,64,512]{2,1,0:T(8,128)(2,1)} %features_ref.1) | copy-start | bytes 786436
